TPU v7x, 32 devices: a whole 2x2x4 slice. The times are simulated.
32 devices in a mesh: grp: 2 (over x), res: 16 (over z, y, core).
Axes of the slice: x: 2, y: 2, z: 4, core: 2. Of those that a mesh axis runs over, the one named last changes fastest.
Arguments:
- alignment_activations: bfloat16 [128, 128, 256], P('grp', 'res'), parts along dimension 0, may hold values from -6 to 6
- projection_weight: bfloat16 [256, 64], replicated, may hold values from -0.375 to 0.375
- output_weight: bfloat16 [1024, 128], replicated, may hold values from -0.1875 to 0.1875
- output_bias: float32 [128], replicated, may hold values from -3 to 3
- pair_update_gradient: bfloat16 [256, 128, 128], P(('grp', 'res')), parts along dimension 0, may hold values from -6 to 6
- sequence_mask: int32 [128], P('grp'), parts along dimension 0, may hold values 0 or 1
- residue_mask: int32 [256], P('grp'), parts along dimension 0, may hold values 0 or 1
Outputs:
- pair_increment: bfloat16 [256, 128, 128], P(('grp', 'res')), parts along dimension 0
- alignment_gradient: bfloat16 [128, 128, 256], P('grp', 'res'), parts along dimension 0
There are 2 independent parts, one for each index of `grp`. A program takes and returns all parts, laid end to end along the dimension named above; an argument that names none is the same for every part. Nothing has to cross between parts.
All inputs are finite; a program needn't handle non-finite values.
Results may differ from a plain program's by a relative error of at most 0.007.
Values may be sent and summed in bfloat16 or wider, within the bound.
A program may use at most 64 MiB of HBM per device.

v0:
```python
import jax
import jax.numpy as jnp
from jax import lax
from jax.sharding import PartitionSpec as P

eps_norm = 1e-05


def layer_norm_forward(values):
    mean_val = jnp.mean(values, axis=-1, keepdims=True)
    centered = values - mean_val
    inverse_deviation = lax.rsqrt(jnp.mean(centered * centered, axis=-1, keepdims=True) + eps_norm)
    return (centered * inverse_deviation, inverse_deviation)


def layer_norm_backward(grad_out, scaled_product, inverse_deviation):
    mean_grad = jnp.mean(grad_out, axis=-1, keepdims=True)
    mean_cross = jnp.mean(grad_out * scaled_product, axis=-1, keepdims=True)
    return inverse_deviation * (grad_out - mean_grad - scaled_product * mean_cross)


def body(
    alignment_activations,
    projection_weight,
    output_weight,
    output_bias,
    pair_update_gradient,
    sequence_mask,
    residue_mask,
):
    alignment_rows = alignment_activations.shape[0]
    local_rows = alignment_activations.shape[1]
    alignment_width = alignment_activations.shape[2]
    projected_width = projection_weight.shape[1] // 2
    pair_width = output_weight.shape[1]
    row_start = lax.axis_index("res") * local_rows
    residue_float_mask = residue_mask.astype(jnp.float32)
    local_residues = lax.dynamic_slice_in_dim(residue_float_mask, row_start, local_rows)
    alignment_mask = sequence_mask.astype(jnp.float32)[:, None] * local_residues[None, :]
    scaled_product, inverse_deviation = layer_norm_forward(
        alignment_activations.astype(jnp.float32)
    )
    normalized_input = scaled_product.astype(jnp.bfloat16)
    projected_rows = jnp.dot(
        normalized_input.reshape(-1, alignment_width),
        projection_weight,
        preferred_element_type=jnp.float32,
    )
    projected_rows = (
        projected_rows.reshape(alignment_rows, local_rows, 2 * projected_width)
        * alignment_mask[:, :, None]
    )
    projected_rows = projected_rows.astype(jnp.bfloat16)
    left_projected = projected_rows[:, :, :projected_width]
    right_proj = projected_rows[:, :, projected_width:]
    live_rows = jnp.sum(sequence_mask.astype(jnp.float32))
    right_all = lax.all_gather(right_proj, "res", axis=1, tiled=True)
    residue_count = right_all.shape[1]
    block_columns = 256 if residue_count % 256 == 0 else residue_count
    block_count = residue_count // block_columns
    count_rows = jnp.maximum(live_rows * local_residues[:, None] * residue_float_mask[None, :], 1.0)

    def pair_block(carry, block_id):
        pair_increment, left_gradient, gradient_pieces = carry
        column_offset = block_id * block_columns
        right_blk = lax.dynamic_slice_in_dim(right_all, column_offset, block_columns, 1)
        cot_blk = lax.dynamic_slice_in_dim(pair_update_gradient, column_offset, block_columns, 1)
        count_blk = lax.dynamic_slice_in_dim(count_rows, column_offset, block_columns, 1)
        outer = jnp.einsum(
            "sic,sjd->ijcd", left_projected, right_blk, preferred_element_type=jnp.float32
        )
        outer = outer.astype(jnp.bfloat16).reshape(-1, projected_width * projected_width)
        update = jnp.dot(outer, output_weight, preferred_element_type=jnp.float32)
        update = update.reshape(local_rows, block_columns, pair_width) + output_bias
        update = (update / count_blk[:, :, None]).astype(jnp.bfloat16)
        pair_increment = lax.dynamic_update_slice_in_dim(pair_increment, update, column_offset, 1)
        grad_outer = jnp.dot(
            cot_blk.reshape(-1, pair_width), output_weight.T, preferred_element_type=jnp.float32
        )
        grad_outer = (
            grad_outer.reshape(local_rows, block_columns, projected_width, projected_width)
            / count_blk[:, :, None, None]
        )
        grad_outer = grad_outer.astype(jnp.bfloat16)
        left_gradient = left_gradient + jnp.einsum(
            "ijcd,sjd->sic", grad_outer, right_blk, preferred_element_type=jnp.float32
        )
        gradient_piece = jnp.einsum(
            "ijcd,sic->jsd", grad_outer, left_projected, preferred_element_type=jnp.float32
        )
        gradient_pieces = lax.dynamic_update_slice_in_dim(
            gradient_pieces,
            gradient_piece.reshape(block_columns, alignment_rows * projected_width),
            column_offset,
            0,
        )
        return ((pair_increment, left_gradient, gradient_pieces), None)

    start_update = jnp.zeros((local_rows, residue_count, pair_width), jnp.bfloat16)
    initial_left = jnp.zeros((alignment_rows, local_rows, projected_width), jnp.float32)
    initial_pieces = jnp.zeros((residue_count, alignment_rows * projected_width), jnp.float32)
    (pair_increment, left_gradient, gradient_pieces), unused = lax.scan(
        pair_block, (start_update, initial_left, initial_pieces), jnp.arange(block_count)
    )
    gradient_total = lax.psum_scatter(gradient_pieces, "res", scatter_dimension=0, tiled=True)
    right_gradient = gradient_total.reshape(local_rows, alignment_rows, projected_width).transpose(
        1, 0, 2
    )
    projection_gradient = (
        jnp.concatenate([left_gradient, right_gradient], axis=-1) * alignment_mask[:, :, None]
    )
    projection_gradient = projection_gradient.astype(jnp.bfloat16)
    normalized_gradient = jnp.dot(
        projection_gradient.reshape(-1, 2 * projected_width),
        projection_weight.T,
        preferred_element_type=jnp.float32,
    )
    normalized_gradient = normalized_gradient.reshape(alignment_rows, local_rows, alignment_width)
    alignment_gradient = layer_norm_backward(
        normalized_gradient, scaled_product, inverse_deviation
    ).astype(jnp.bfloat16)
    return (pair_increment, alignment_gradient)


def solution(mesh):
    in_specs = (
        P("grp", "res", None),
        P(),
        P(),
        P(),
        P(("grp", "res"), None, None),
        P("grp"),
        P("grp"),
    )
    out_specs = (P(("grp", "res"), None, None), P("grp", "res", None))
    return jax.shard_map(body, mesh=mesh, in_specs=in_specs, out_specs=out_specs, check_vma=False)
```

profile of v0, /device:TPU:0, one launch (start us, length us, event | category | flops | bytes accessed | tf_op | source)
XLA Modules:
  0.0 89.5 jit_solution(17013610262894951195)
XLA Ops:
  7.2 0.0 copy-start
  7.2 0.0 reduce-scatter.4.cloned.1.call-start
  7.2 1.3 %convert_reduce_fusion.1 = f32[]{:T(128)} fusion(s32[64]{0:T(128)} %param.12), kind=kLoop, calls=%fused_computation.46 | loop fusion | flops 127 | bytes 260 | tf_op jit(solution)/shard_map/reduce_sum | solution.py:56
  8.5 0.7 convert_element_type.41
  9.2 0.7 convert_element_type.42
  9.9 1.1 %convert_reduce_fusion = f32[64,8]{1,0:T(8,128)S(1)} fusion(bf16[64,8,256]{2,1,0:T(8,128)(2,1)} %param.7), kind=kLoop, calls=%fused_computation.15 | loop fusion | flops 261632 | bytes 264192 | tf_op jit(solution)/shard_map/reduce_sum | solution.py:10
  11.0 1.2 %fusion.23 = f32[64,8]{1,0:T(8,128)S(1)} fusion(bf16[64,8,256]{2,1,0:T(8,128)(2,1)} %param.7, f32[64,8]{1,0:T(8,128)S(1)} %broadcast_multiply_fusion.3), kind=kLoop, calls=%fused_computation.25 | loop fusion | flops 523776 | bytes 266240 | tf_op jit(solution)/shard_map/reduce_sum | solution.py:12
  12.2 0.7 broadcast_multiply_fusion.4
  12.9 0.1 add_rsqrt_fusion
  13.0 0.6 copy-done.4
  13.6 1.3 %fusion.9 = bf16[64,8,64]{2,1,0:T(8,128)(2,1)S(1)} fusion(bf16[64,8,256]{2,1,0:T(8,128)(2,1)} %param.7, f32[64,8]{1,0:T(8,128)S(1)} %get-tuple-element.29, f32[64,8]{1,0:T(8,128)S(1)} %broadcast_multiply_fusion.3, f32[64,8]{1,0:T(8,128)S(1)} %get-tuple-element.40, bf16[256,64]{0,1:T(8,128)(2,1)} %param.8), kind=kOutput, calls=%fused_computation.11 | convolution fusion | flops 17367040 | bytes 366592 | tf_op jit(solution)/shard_map/dot_general | solution.py:44
  14.8 0.1 fusion.39
  14.9 0.1 copy.23
  15.1 0.1 multiply_maximum_fusion
  15.2 0.7 divide_convert_fusion
  15.9 0.8 fusion.4
  16.7 0.6 copy.30
  17.3 1.3 %copy.43 = f32[128,2048]{1,0:T(8,128)} copy(f32[128,2048]{0,1:T(8,128)S(1)} %bitcast.49) | data formatting | bytes 2097152
  18.6 0.0 reduce-scatter.4.cloned.1.call-update
  18.7 32.2 %all_gather.3 = bf16[64,128,32]{2,1,0:T(8,128)(2,1)S(1)} all-gather(bf16[64,8,32]{2,1,0:T(8,128)(2,1)S(1)} %get-tuple-element.27), channel_id=1, replica_groups=mesh['grp'=2,'res'=16] {'res'}, dimensions={1}, use_global_device_ids=true | all-gather | bytes 557056 | tf_op jit(solution)/shard_map/all_gather | solution.py:57
  50.9 3.2 %copy.26 = bf16[64,128,32]{0,1,2:T(8,128)(2,1)S(1)} copy(bf16[64,128,32]{2,1,0:T(8,128)(2,1)S(1)} %all_gather.3) | data formatting | bytes 1048576 | tf_op jit(solution)/shard_map/all_gather | solution.py:57
  54.1 3.0 %fusion.10 = f32[64,8,32]{0,2,1:T(8,128)} fusion(bf16[8,128,32,32]{1,3,2,0:T(8,128)(2,1)} %copy-done.2, bf16[64,128,32]{0,1,2:T(8,128)(2,1)S(1)} %copy.26), kind=kOutput, calls=%fused_computation.12 | convolution fusion | flops 134217728 | bytes 2686976 | tf_op jit(solution)/shard_map/while/body/eval_jaxpr/ijcd,sjd->sic/dot_general | solution.py:85
  57.1 1.7 %copy.33 = f32[64,8,32]{2,1,0:T(8,128)} copy(f32[64,8,32]{0,2,1:T(8,128)} %fusion.10) | data formatting | bytes 131072 | tf_op jit(solution)/shard_map/while/body/eval_jaxpr/ijcd,sjd->sic/dot_general | solution.py:85
  58.8 3.2 %copy.34 = bf16[64,128,32,1]{0,1,3,2:T(8,128)(2,1)S(1)} copy(bf16[64,128,32,1]{2,1,0,3:T(8,128)(2,1)S(1)} %bitcast.47) | data formatting | bytes 1048576 | tf_op jit(solution)/shard_map/all_gather | solution.py:57
  62.0 0.7 convert_bitcast_fusion
  62.7 1.4 %copy.24 = bf16[8,128,32,32]{1,3,2,0:T(8,128)(2,1)S(1)} copy(bf16[8,128,32,32]{1,2,0,3:T(8,128)(2,1)S(1)} %convert_bitcast_fusion) | data formatting | bytes 4194304 | tf_op jit(solution)/shard_map/while/body/eval_jaxpr/convert_element_type | solution.py:72
  64.1 1.5 %fusion.8 = bf16[8,128,128]{2,1,0:T(8,128)(2,1)} fusion(bf16[8,128,1024]{1,2,0:T(8,128)(2,1)S(1)} %bitcast.50, bf16[1024,128]{1,0:T(8,128)(2,1)S(1)} %copy-done, f32[8,128]{1,0:T(8,128)S(1)} %multiply_maximum_fusion, f32[128]{0:T(128)S(1)} %copy-done.8), kind=kOutput, calls=%fused_computation.9 | convolution fusion | flops 268828672 | bytes 2626048 | tf_op jit(solution)/shard_map/while/body/eval_jaxpr/dot_general | solution.py:73
  65.6 13.9 %reduce-scatter.4.cloned.1.call-done = f32[8,2048]{1,0:T(8,128)} async-done(((f32[128,2048]{1,0:T(8,128)}), f32[8,2048]{1,0:T(8,128)}) %reduce-scatter.4.cloned.1.call-update) | async-done | bytes 65552
  79.5 1.2 %copy.44 = f32[8,2048]{0,1:T(8,128)S(1)} copy(f32[8,2048]{1,0:T(8,128)} %reduce-scatter.4.cloned.1.call-done) | data formatting | bytes 131072
  80.7 0.3 copy.32
  81.0 0.5 fusion.38
  81.6 1.0 %fusion.22 = bf16[64,8,256]{2,1,0:T(8,128)(2,1)} fusion(bf16[64,8,256]{2,1,0:T(8,128)(2,1)S(1)} %copy-done.1, f32[64,8,256]{2,1,0:T(8,128)S(1)} %get-tuple-element.28, f32[64,8]{1,0:T(8,128)S(1)} %broadcast_multiply_fusion.1, f32[64,8]{1,0:T(8,128)S(1)} %broadcast_multiply_fusion.2, f32[64,8]{1,0:T(8,128)S(1)} %get-tuple-element.29, ...), kind=kLoop, calls=%fused_computation.24 | loop fusion | flops 1048576 | bytes 1056768 | tf_op jit(solution)/shard_map/convert_element_type | solution.py:121
  (19 shorter events, 0.0 us)
Async XLA Ops:
  7.2 8.0 %copy-start = (bf16[1024,128]{1,0:T(8,128)(2,1)S(1)}, bf16[1024,128]{1,0:T(8,128)(2,1)}, u32[]{:S(2)}) copy-start(bf16[1024,128]{1,0:T(8,128)(2,1)} %param.9) | copy-start | bytes 786436
  7.2 8.0 %copy-start.7 = (bf16[8,128,128]{2,1,0:T(8,128)(2,1)S(1)}, bf16[8,128,128]{2,1,0:T(8,128)(2,1)}, u32[]{:S(2)}) copy-start(bf16[8,128,128]{2,1,0:T(8,128)(2,1)} %param.11) | copy-start | bytes 786436
  7.2 72.3 %reduce-scatter.4.cloned.1.call-start = ((), (), s32[]{:S(2)}) async-start(), calls=%async_computation.1 | async-start | bytes 1114112
  13.0 0.6 copy-start.4
  15.9 1.4 %copy-start.2 = (bf16[8,128,32,32]{1,3,2,0:T(8,128)(2,1)}, bf16[8,128,32,32]{1,3,2,0:T(8,128)(2,1)S(1)}, u32[]{:S(2)}) copy-start(bf16[8,128,32,32]{1,3,2,0:T(8,128)(2,1)S(1)} %divide_convert_fusion) | copy-start | bytes 6291460
  62.7 1.4 %copy-start.8 = (f32[128]{0:T(128)S(1)}, f32[128]{0:T(128)}, u32[]{:S(2)}) copy-start(f32[128]{0:T(128)} %param.10) | copy-start | bytes 1540
  65.6 15.4 %copy-start.1 = (bf16[64,8,256]{2,1,0:T(8,128)(2,1)S(1)}, bf16[64,8,256]{2,1,0:T(8,128)(2,1)}, u32[]{:S(2)}) copy-start(bf16[64,8,256]{2,1,0:T(8,128)(2,1)} %param.7) | copy-start | bytes 786436
  65.6 15.4 %copy-start.3 = (f32[64,8,32]{2,1,0:T(8,128)S(1)}, f32[64,8,32]{2,1,0:T(8,128)}, u32[]{:S(2)}) copy-start(f32[64,8,32]{2,1,0:T(8,128)} %copy.33) | copy-start | bytes 196612
  65.6 15.4 %copy-start.5 = (f32[64,8]{1,0:T(8,128)S(1)}, f32[64,8]{1,0:T(8,128)}, u32[]{:S(2)}) copy-start(f32[64,8]{1,0:T(8,128)} %copy-done.4) | copy-start | bytes 6148
  65.6 15.4 %copy-start.6 = (bf16[256,64]{0,1:T(8,128)(2,1)S(1)}, bf16[256,64]{0,1:T(8,128)(2,1)}, u32[]{:S(2)}) copy-start(bf16[256,64]{0,1:T(8,128)(2,1)} %param.8) | copy-start | bytes 98308
Sparse Core Ops, SparseCore 0:
  18.8 60.6 reduce-scatter.3
where the time goes:
time: 89.8 us; the launch traced here: 89.5 us
  blocking collectives  32.2 us (36%)
  between operations  14.2 us (16%)
  waiting for transfers between devices  13.9 us (15%)
  local copies, waits for them, and re-layouts  13.8 us (15%)
  matrix products  8.48 us (9%)
  other arithmetic  6.82 us (8%)
    all_gather x1, blocking collectives, body(): right_all = lax.all_gather(right_proj, 'res', axis=1, tiled=True)  32.2 us
    unnamed x2, waiting for transfers between devices  13.9 us
    all_gather x2, local copies, waits for them, and re-layouts, body(): right_all = lax.all_gather(right_proj, 'res', axis=1, tiled=True)  6.35 us
    unnamed x20, local copies, waits for them, and re-layouts  3.13 us
    dot_general x1, matrix products, pair_block(): jnp.einsum('ijcd,sjd->sic', grad_outer, right_blk, preferred_element_type...  2.99 us
  transfers between devices with their start and end apart: 1, of which 1 were waited for; matrix products, arithmetic and copies ran while one was open for 16% of the time, Pallas kernels for 0%

commit v1 on v0

v1 whole, which is shorter than its diff:
```python
import functools

import jax
import jax.numpy as jnp
from jax import lax
from jax.experimental import pallas as pl
from jax.experimental.pallas import tpu as pltpu
from jax.sharding import PartitionSpec as P

EPS = 1e-05
MESH = pl.DeviceIdType.MESH
F32 = jnp.float32
BF16 = jnp.bfloat16


def dot(a, b, ca, cb):
    return lax.dot_general(a, b, (((ca,), (cb,)), ((), ())), preferred_element_type=F32)


def kernel(
    n,
    x_ref,
    wp_ref,
    wo_ref,
    bias_ref,
    g_ref,
    seq_ref,
    res_ref,
    res_smem,
    upd_ref,
    out_ref,
    scaled_ref,
    inv_ref,
    wide_ref,
    wf_ref,
    w_ref,
    tr_ref,
    lw_ref,
    gm_ref,
    ra_ref,
    r_ref,
    rall_ref,
    part_ref,
    sib_ref,
    red_ref,
    rsin_ref,
    ag_send,
    ag_recv,
    fw_send,
    fw_recv,
    sib_sem,
    rs_send,
    rs_recv,
):
    S, L, C = x_ref.shape
    D = wp_ref.shape[1] // 2
    Q = wo_ref.shape[1]
    H = D // 2
    K = D * S
    R = g_ref.shape[1]
    nchip = n // 2
    me = lax.axis_index("res")
    kind = lax.rem(me, 2)
    chip = lax.div(me, 2)
    sibling = me + 1 - 2 * kind

    def peer(o):
        return lax.rem(chip + o, nchip) * 2 + kind

    def source(o):
        return lax.rem(chip + nchip - o, nchip)

    barrier = pltpu.get_barrier_semaphore()
    pl.semaphore_signal(barrier, inc=1, device_id={"res": sibling}, device_id_type=MESH)
    for o in range(1, nchip):
        pl.semaphore_signal(barrier, inc=1, device_id={"res": peer(o)}, device_id_type=MESH)

    seq_row = seq_ref[...].astype(F32)
    res_row = res_ref[...].astype(F32)
    live = jnp.sum(seq_row, axis=1, keepdims=True)
    same = lax.broadcasted_iota(jnp.int32, (S, S), 0) == lax.broadcasted_iota(jnp.int32, (S, S), 1)
    seq_col = jnp.sum(jnp.where(same, seq_row, 0.0), axis=1, keepdims=True)
    res_mine = [res_smem[me * L + j].astype(F32) for j in range(L)]

    x = x_ref[...].astype(F32).reshape(S * L, C)
    mean = jnp.mean(x, axis=1, keepdims=True)
    centered = x - mean
    inv = lax.rsqrt(jnp.mean(centered * centered, axis=1, keepdims=True) + EPS)
    scaled = centered * inv
    inv_ref[...] = jnp.broadcast_to(inv, inv_ref.shape)
    lanes = C // 2
    for h in range(2):
        scaled_ref[h] = scaled[:, h * lanes : (h + 1) * lanes]

    wp = wp_ref[...]
    w_left = wp[:, :D]
    wp_t = jnp.transpose(
        jnp.concatenate([wp.astype(F32), jnp.zeros((C, 128 - 2 * D), F32)], axis=1)
    ) if 2 * D < 128 else jnp.transpose(wp.astype(F32))
    wl_t = wp_t[:D].astype(BF16)
    wr_t = wp_t[D : 2 * D].astype(BF16)
    lefts = []
    for j in range(L):
        rows = jnp.concatenate(
            [scaled_ref[h, pl.ds(j, S, stride=L), :] for h in range(2)], axis=1
        )
        rows = (rows * (seq_col * res_mine[j])).astype(BF16)
        lefts.append(dot(rows, w_left, 1, 0).astype(BF16))
        twice = jnp.concatenate([rows, rows], axis=0)
        tr_ref[j * D : (j + 1) * D, :] = dot(wr_t, twice, 1, 1)
    left = jnp.concatenate(lefts, axis=0)
    first = lax.broadcasted_iota(jnp.int32, (L, 2 * S), 1) < S
    blocks = [
        jnp.where(first, tr_ref[pl.ds(v, L, stride=D), :], tr_ref[pl.ds(H + v, L, stride=D), :])
        for v in range(H)
    ]
    half = jnp.concatenate(blocks[: H // 2], axis=1), jnp.concatenate(blocks[H // 2 :], axis=1)
    rall_ref[kind, chip] = jnp.concatenate(half, axis=0).astype(BF16)

    pl.semaphore_wait(barrier, nchip)

    def gather(o):
        mine = rall_ref.at[kind, chip]
        return pltpu.make_async_remote_copy(
            mine, mine, ag_send.at[o], ag_recv.at[o], device_id={"res": peer(o)}, device_id_type=MESH
        )

    def gathered(o):
        got = rall_ref.at[kind, source(o)]
        return pltpu.make_async_remote_copy(
            got, got, ag_send.at[o], ag_recv.at[o], device_id={"res": peer(o)}, device_id_type=MESH
        )

    def forward(o):
        slab = rall_ref.at[kind, source(o)]
        return pltpu.make_async_remote_copy(
            slab, slab, fw_send.at[o], fw_recv.at[o], device_id={"res": sibling}, device_id_type=MESH
        )

    def forwarded(o):
        slab = rall_ref.at[1 - kind, source(o)]
        return pltpu.make_async_remote_copy(
            slab, slab, fw_send.at[o], fw_recv.at[o], device_id={"res": sibling}, device_id_type=MESH
        )

    for o in range(1, nchip):
        gather(o).start()
    forward(0).start()

    wf_ref[...] = wo_ref[...].astype(F32)
    for v in range(H):
        for e in range(2):
            w_ref[:, (2 * v + e) * Q : (2 * v + e + 1) * Q] = wf_ref[
                pl.ds(e * H + v, D, stride=D), :
            ].astype(BF16)
    for i in range(L):
        gm_ref[:, i * Q : (i + 1) * Q] = g_ref[i]

    for v in range(H):
        lw = dot(left, w_ref[:, 2 * v * Q : (2 * v + 2) * Q], 1, 0).astype(BF16)
        for e in range(2):
            for i in range(L):
                lw_ref[(2 * v + e) * S : (2 * v + e + 1) * S, i * Q : (i + 1) * Q] = lw[
                    i * S : (i + 1) * S, e * Q : (e + 1) * Q
                ]

    KH = K // 2
    step = 256
    for t in range(KH // step):
        pieces = [
            dot(gm_ref[...], lw_ref[h * KH + t * step : h * KH + (t + 1) * step, :], 1, 1).reshape(
                nchip, 2, L, step
            )
            for h in range(2)
        ]
        for kd in range(2):
            both = jnp.concatenate([pieces[0][:, kd], pieces[1][:, kd]], axis=1)
            part_ref[kd, :, :, t * step : (t + 1) * step] = both.astype(BF16)

    pair = pltpu.make_async_remote_copy(
        part_ref.at[1 - kind],
        sib_ref,
        sib_sem.at[0],
        sib_sem.at[1],
        device_id={"res": sibling},
        device_id_type=MESH,
    )
    pair.start()
    for o in range(1, nchip):
        gathered(o).wait_recv()
        forward(o).start()
    pair.wait_recv()
    red_ref[...] = (part_ref[kind].astype(F32) + sib_ref[...].astype(F32)).astype(BF16)

    def scatter(o):
        return pltpu.make_async_remote_copy(
            red_ref.at[lax.rem(chip + o, nchip)],
            rsin_ref.at[o],
            rs_send.at[o],
            rs_recv.at[o],
            device_id={"res": peer(o)},
            device_id_type=MESH,
        )

    for o in range(1, nchip):
        scatter(o).start()
    for o in range(nchip):
        forwarded(o).wait_recv()

    for h in range(2):
        kinds = [
            rall_ref[kd].astype(F32)[:, h * L : (h + 1) * L, :].reshape(nchip, 1, L, KH)
            for kd in range(2)
        ]
        ra_ref[:, h * KH : (h + 1) * KH] = (
            jnp.concatenate(kinds, axis=1).reshape(R, KH).astype(BF16)
        )

    for v in range(H):
        r = dot(ra_ref[:, v * 2 * S : (v + 1) * 2 * S], gm_ref[...], 0, 0).astype(BF16)
        for e in range(2):
            for i in range(L):
                r_ref[i * S : (i + 1) * S, (2 * v + e) * Q : (2 * v + e + 1) * Q] = r[
                    e * S : (e + 1) * S, i * Q : (i + 1) * Q
                ]
    left_grad = dot(r_ref[...], w_ref[...], 1, 1).astype(BF16)

    same_r = lax.broadcasted_iota(jnp.int32, (R, R), 0) == lax.broadcasted_iota(
        jnp.int32, (R, R), 1
    )
    res_col = jnp.sum(jnp.where(same_r, res_row, 0.0), axis=1, keepdims=True)
    live_col = live * res_col
    bias = bias_ref[...]
    for b in range(L // 2):
        u = dot(ra_ref[...], lw_ref[:, 2 * b * Q : (2 * b + 2) * Q], 1, 0)
        for e in range(2):
            i = 2 * b + e
            factor = 1.0 / jnp.maximum(live_col * res_mine[i], 1.0)
            upd_ref[i] = ((u[:, e * Q : (e + 1) * Q] + bias) * factor).astype(BF16)

    total = red_ref[chip].astype(F32)
    for o in range(1, nchip):
        scatter(o).wait_recv()
        total = total + rsin_ref[o].astype(F32)
    for v in range(H):
        h, u = v // (H // 2), v % (H // 2)
        tr_ref[pl.ds(v, L, stride=H), :] = total[h * L : (h + 1) * L, u * 2 * S : (u + 1) * 2 * S]

    inv_live = 1.0 / jnp.maximum(live, 1.0)
    seq_scale = seq_col * inv_live
    for j in range(L):
        piece = tr_ref[j * H : (j + 1) * H, :]
        right_t = jnp.concatenate([piece[:, :S], piece[:, S:]], axis=0).astype(BF16)
        gn = dot(left_grad[j * S : (j + 1) * S], wl_t, 1, 0) + dot(right_t, wr_t, 0, 0)
        gn = gn * (seq_scale * res_mine[j])
        for h in range(2):
            wide_ref[h, pl.ds(j, S, stride=L), :] = gn[:, h * lanes : (h + 1) * lanes]

    gn = jnp.concatenate([wide_ref[0], wide_ref[1]], axis=1)
    sc = jnp.concatenate([scaled_ref[0], scaled_ref[1]], axis=1)
    mean_g = jnp.mean(gn, axis=1, keepdims=True)
    mean_c = jnp.mean(gn * sc, axis=1, keepdims=True)
    result = inv_ref[:, :1] * (gn - mean_g - sc * mean_c)
    out_ref[...] = result.reshape(S, L, C).astype(BF16)

    for o in range(1, nchip):
        gather(o).wait_send()
        scatter(o).wait_send()
    for o in range(nchip):
        forward(o).wait_send()
    pair.wait_send()


def body(n, x, wp, wo, bias, g, seq, res):
    S, L, C = x.shape
    D = wp.shape[1] // 2
    Q = wo.shape[1]
    R = g.shape[1]
    K = D * S
    nchip = n // 2
    vm = pl.BlockSpec(memory_space=pltpu.VMEM)
    dma = pltpu.SemaphoreType.DMA
    slab = (2 * L, K // 2)
    return pl.pallas_call(
        functools.partial(kernel, n),
        out_shape=(
            jax.ShapeDtypeStruct((L, R, Q), BF16),
            jax.ShapeDtypeStruct((S, L, C), BF16),
        ),
        in_specs=[vm] * 7 + [pl.BlockSpec(memory_space=pltpu.SMEM)],
        out_specs=(vm, vm),
        scratch_shapes=[
            pltpu.VMEM((2, S * L, C // 2), F32),
            pltpu.VMEM((S * L, 128), F32),
            pltpu.VMEM((2, S * L, C // 2), F32),
            pltpu.VMEM((D * D, Q), F32),
            pltpu.VMEM((D, D * Q), BF16),
            pltpu.VMEM((L * D, 2 * S), F32),
            pltpu.VMEM((K, L * Q), BF16),
            pltpu.VMEM((R, L * Q), BF16),
            pltpu.VMEM((R, K), BF16),
            pltpu.VMEM((S * L, D * Q), BF16),
            pltpu.VMEM((2, nchip) + slab, BF16),
            pltpu.VMEM((2, nchip) + slab, BF16),
            pltpu.VMEM((nchip,) + slab, BF16),
            pltpu.VMEM((nchip,) + slab, BF16),
            pltpu.VMEM((nchip,) + slab, BF16),
            dma((nchip,)),
            dma((nchip,)),
            dma((nchip,)),
            dma((nchip,)),
            dma((2,)),
            dma((nchip,)),
            dma((nchip,)),
        ],
        compiler_params=pltpu.CompilerParams(
            collective_id=0, has_side_effects=True, vmem_limit_bytes=56 * 1024 * 1024
        ),
    )(x, wp, wo, bias.reshape(1, -1), g, seq.reshape(1, -1), res.reshape(1, -1), res)


def solution(mesh):
    in_specs = (
        P("grp", "res", None),
        P(),
        P(),
        P(),
        P(("grp", "res"), None, None),
        P("grp"),
        P("grp"),
    )
    out_specs = (P(("grp", "res"), None, None), P("grp", "res", None))
    return jax.shard_map(
        functools.partial(body, mesh.shape["res"]),
        mesh=mesh,
        in_specs=in_specs,
        out_specs=out_specs,
        check_vma=False,
    )
```

time: 89.8 us -> 26.2 us (0.29)
  blocking collectives: 32.2 us -> 0 us
  Pallas kernels: 0 us -> 21.4 us
  waiting for transfers between devices: 13.9 us -> 0 us
  between operations: 14.2 us -> 0.65 us
  local copies, waits for them, and re-layouts: 13.8 us -> 3.91 us
  matrix products: 8.48 us -> 0 us
  other arithmetic: 6.82 us -> 0 us
    all_gather x1 -> x0, blocking collectives: 32.2 us -> none  [body(): right_all = lax.all_gather(right_proj, 'res', axis=1, tiled=True)]
    pallas_call x0 -> x1, Pallas kernels: none -> 21.4 us  [body(): pl.pallas_call(functools.partial(kernel, n), out_shape=(jax.ShapeDtypeStr...]
    unnamed x2 -> x0, waiting for transfers between devices: 13.9 us -> none
    dot_general x7 -> x0, matrix products: 8.48 us -> none  [the longest x1 2.99 us: pair_block(): jnp.einsum('ijcd,sjd->sic', grad_outer, right_blk, preferred_element_type...]
    all_gather x2 -> x0, local copies, waits for them, and re-layouts: 6.35 us -> none  [body(): right_all = lax.all_gather(right_proj, 'res', axis=1, tiled=True)]
    reduce_sum x3 -> x0, other arithmetic: 3.57 us -> none  [the longest x1 1.31 us: body(): live_rows = jnp.sum(sequence_mask.astype(jnp.float32))]
    convert_element_type x3 -> x0, other arithmetic: 2.36 us -> none  [the longest x1 1.05 us: body(): alignment_gradient = layer_norm_backward(normalized_gradient, scaled_prod...]
    dot_general x1 -> x0, local copies, waits for them, and re-layouts: 1.74 us -> none  [pair_block(): jnp.einsum('ijcd,sjd->sic', grad_outer, right_blk, preferred_element_type...]
  transfers between devices with their start and end apart: 1 -> 0, of which waited for: 1 -> 0; matrix products, arithmetic and copies ran while one was open for 16% -> 0% of each run, Pallas kernels for 0% -> 0%
where the time goes in v1:
time: 26.2 us; the launch traced here: 25.9 us
  Pallas kernels  21.4 us (82%)
  local copies, waits for them, and re-layouts  3.91 us (15%)
  between operations  0.65 us (2%)
    pallas_call x1, Pallas kernels, body(): pl.pallas_call(functools.partial(kernel, n), out_shape=(jax.ShapeDtypeStr...  21.4 us
    unnamed x5, local copies, waits for them, and re-layouts  3.91 us

profile of v1, /device:TPU:0, one launch (start us, length us, event | category | flops | bytes accessed | tf_op | source)
XLA Modules:
  0.0 25.9 jit_solution(2772603084433356722)
XLA Ops:
  0.6 1.5 %copy.9.wp_ref = bf16[256,64]{1,0:T(8,128)(2,1)} copy(bf16[256,64]{0,1:T(8,128)(2,1)} %param.8) | data formatting | bytes 65536 | tf_op args[1]
  2.1 21.4 %shard_map.86 = (bf16[8,128,128]{2,1,0:T(8,128)(2,1)}, bf16[64,8,256]{2,1,0:T(8,128)(2,1)}) custom-call(bf16[64,8,256]{2,1,0:T(8,128)(2,1)} %x_ref.1, bf16[256,64]{1,0:T(8,128)(2,1)} %copy.9.wp_ref, bf16[1024,128]{1,0:T(8,128)(2,1)} %wo_ref.1, f32[1,128]{1,0:T(1,128)} %bitcast.4, bf16[8,128,128]{2,1,0:T(8,128)(2,1)} %g_ref.1, s32[1,64]{1,0:T(1,128)} %bitcast.5, ...), custom_call_target="tpu_custom_call" | custom-call | tf_op jit(solution)/shard_map/pallas_call | solution.py:284
  23.5 0.0 copy-start
  23.5 1.7 %copy.12 = bf16[8,128,128]{2,1,0:T(8,128)(2,1)} copy(bf16[8,128,128]{2,1,0:T(8,128)(2,1)} %get-tuple-element.4) | data formatting | bytes 524288
  25.2 0.0 copy-done
  25.2 0.7 %copy.13 = bf16[64,8,256]{2,1,0:T(8,128)(2,1)} copy(bf16[64,8,256]{2,1,0:T(8,128)(2,1)S(1)} %copy-done) | data formatting | bytes 524288
Async XLA Ops:
  23.5 1.7 %copy-start = (bf16[64,8,256]{2,1,0:T(8,128)(2,1)S(1)}, bf16[64,8,256]{2,1,0:T(8,128)(2,1)}, u32[]{:S(2)}) copy-start(bf16[64,8,256]{2,1,0:T(8,128)(2,1)} %get-tuple-element.5) | copy-start | bytes 786436

commit v2 on v1

--- a/solution.py
+++ b/solution.py
@@ -21,17 +21,18 @@
     n,
     x_ref,
     wp_ref,
-    wo_ref,
+    wo_hbm,
     bias_ref,
-    g_ref,
+    g_hbm,
     seq_ref,
     res_ref,
     res_smem,
     upd_ref,
-    out_ref,
     scaled_ref,
     inv_ref,
     wide_ref,
+    g_ref,
+    wo_ref,
     wf_ref,
     w_ref,
     tr_ref,
@@ -51,9 +52,10 @@
     sib_sem,
     rs_send,
     rs_recv,
+    in_sem,
 ):
     S, L, C = x_ref.shape
-    D = wp_ref.shape[1] // 2
+    D = wp_ref.shape[0] // 2
     Q = wo_ref.shape[1]
     H = D // 2
     K = D * S
@@ -70,6 +72,11 @@
     def source(o):
         return lax.rem(chip + nchip - o, nchip)
 
+    load_w = pltpu.make_async_copy(wo_hbm, wo_ref, in_sem.at[0])
+    load_g = pltpu.make_async_copy(g_hbm, g_ref, in_sem.at[1])
+    load_w.start()
+    load_g.start()
+
     barrier = pltpu.get_barrier_semaphore()
     pl.semaphore_signal(barrier, inc=1, device_id={"res": sibling}, device_id_type=MESH)
     for o in range(1, nchip):
@@ -92,20 +99,15 @@
     for h in range(2):
         scaled_ref[h] = scaled[:, h * lanes : (h + 1) * lanes]
 
-    wp = wp_ref[...]
-    w_left = wp[:, :D]
-    wp_t = jnp.transpose(
-        jnp.concatenate([wp.astype(F32), jnp.zeros((C, 128 - 2 * D), F32)], axis=1)
-    ) if 2 * D < 128 else jnp.transpose(wp.astype(F32))
-    wl_t = wp_t[:D].astype(BF16)
-    wr_t = wp_t[D : 2 * D].astype(BF16)
+    wl_t = wp_ref[:D]
+    wr_t = wp_ref[D:]
     lefts = []
     for j in range(L):
         rows = jnp.concatenate(
             [scaled_ref[h, pl.ds(j, S, stride=L), :] for h in range(2)], axis=1
         )
         rows = (rows * (seq_col * res_mine[j])).astype(BF16)
-        lefts.append(dot(rows, w_left, 1, 0).astype(BF16))
+        lefts.append(dot(rows, wl_t, 1, 1).astype(BF16))
         twice = jnp.concatenate([rows, rows], axis=0)
         tr_ref[j * D : (j + 1) * D, :] = dot(wr_t, twice, 1, 1)
     left = jnp.concatenate(lefts, axis=0)
@@ -147,12 +149,14 @@
         gather(o).start()
     forward(0).start()
 
+    load_w.wait()
     wf_ref[...] = wo_ref[...].astype(F32)
     for v in range(H):
         for e in range(2):
             w_ref[:, (2 * v + e) * Q : (2 * v + e + 1) * Q] = wf_ref[
                 pl.ds(e * H + v, D, stride=D), :
             ].astype(BF16)
+    load_g.wait()
     for i in range(L):
         gm_ref[:, i * Q : (i + 1) * Q] = g_ref[i]
 
@@ -256,24 +260,31 @@
         for h in range(2):
             wide_ref[h, pl.ds(j, S, stride=L), :] = gn[:, h * lanes : (h + 1) * lanes]
 
+    for o in range(1, nchip):
+        gather(o).wait_send()
+        scatter(o).wait_send()
+    for o in range(nchip):
+        forward(o).wait_send()
+    pair.wait_send()
+
+
+def finish(upd_ref, scaled_ref, inv_ref, wide_ref, upd_out, out_ref, sem):
+    S, L, C = out_ref.shape
+    copy = pltpu.make_async_copy(upd_ref, upd_out, sem.at[0])
+    copy.start()
     gn = jnp.concatenate([wide_ref[0], wide_ref[1]], axis=1)
     sc = jnp.concatenate([scaled_ref[0], scaled_ref[1]], axis=1)
     mean_g = jnp.mean(gn, axis=1, keepdims=True)
     mean_c = jnp.mean(gn * sc, axis=1, keepdims=True)
     result = inv_ref[:, :1] * (gn - mean_g - sc * mean_c)
     out_ref[...] = result.reshape(S, L, C).astype(BF16)
-
-    for o in range(1, nchip):
-        gather(o).wait_send()
-        scatter(o).wait_send()
-    for o in range(nchip):
-        forward(o).wait_send()
-    pair.wait_send()
+    copy.wait()
 
 
 def body(n, x, wp, wo, bias, g, seq, res):
     S, L, C = x.shape
     D = wp.shape[1] // 2
+    hbm = pl.BlockSpec(memory_space=pl.ANY)
     Q = wo.shape[1]
     R = g.shape[1]
     K = D * S
@@ -281,18 +292,19 @@
     vm = pl.BlockSpec(memory_space=pltpu.VMEM)
     dma = pltpu.SemaphoreType.DMA
     slab = (2 * L, K // 2)
-    return pl.pallas_call(
+    upd, scaled, inv, wide = pl.pallas_call(
         functools.partial(kernel, n),
         out_shape=(
-            jax.ShapeDtypeStruct((L, R, Q), BF16),
-            jax.ShapeDtypeStruct((S, L, C), BF16),
-        ),
-        in_specs=[vm] * 7 + [pl.BlockSpec(memory_space=pltpu.SMEM)],
-        out_specs=(vm, vm),
-        scratch_shapes=[
+            pltpu.VMEM((L, R, Q), BF16),
             pltpu.VMEM((2, S * L, C // 2), F32),
             pltpu.VMEM((S * L, 128), F32),
             pltpu.VMEM((2, S * L, C // 2), F32),
+        ),
+        in_specs=[vm, vm, hbm, vm, hbm, vm, vm] + [pl.BlockSpec(memory_space=pltpu.SMEM)],
+        out_specs=(vm, vm, vm, vm),
+        scratch_shapes=[
+            pltpu.VMEM((L, R, Q), BF16),
+            pltpu.VMEM((D * D, Q), BF16),
             pltpu.VMEM((D * D, Q), F32),
             pltpu.VMEM((D, D * Q), BF16),
             pltpu.VMEM((L * D, 2 * S), F32),
@@ -312,11 +324,23 @@
             dma((2,)),
             dma((nchip,)),
             dma((nchip,)),
+            dma((2,)),
         ],
         compiler_params=pltpu.CompilerParams(
-            collective_id=0, has_side_effects=True, vmem_limit_bytes=56 * 1024 * 1024
+            collective_id=0, has_side_effects=True, vmem_limit_bytes=60 * 1024 * 1024
         ),
-    )(x, wp, wo, bias.reshape(1, -1), g, seq.reshape(1, -1), res.reshape(1, -1), res)
+    )(x, wp.T, wo, bias.reshape(1, -1), g, seq.reshape(1, -1), res.reshape(1, -1), res)
+    return pl.pallas_call(
+        finish,
+        out_shape=(
+            jax.ShapeDtypeStruct((L, R, Q), BF16),
+            jax.ShapeDtypeStruct((S, L, C), BF16),
+        ),
+        in_specs=[vm] * 4,
+        out_specs=(hbm, vm),
+        scratch_shapes=[dma((1,))],
+        compiler_params=pltpu.CompilerParams(vmem_limit_bytes=8 * 1024 * 1024),
+    )(upd, scaled, inv, wide)
 
 
 def solution(mesh):

time: 26.2 us -> 22.5 us (0.86)
  local copies, waits for them, and re-layouts: 3.91 us -> 0 us
  Pallas kernels: 21.4 us -> 21.7 us
    unnamed x5 -> x0, local copies, waits for them, and re-layouts: 3.91 us -> none
    pallas_call x1 -> x2, Pallas kernels: 21.4 us -> 21.7 us  [the longest x1 20.2 us: body(): pl.pallas_call(functools.partial(kernel, n), out_shape=(pltpu.VMEM((L, R,...]
where the time goes in v2:
time: 22.5 us; the launch traced here: 22.3 us
  Pallas kernels  21.7 us (96%)
  between operations  0.64 us (3%)
    pallas_call x1, Pallas kernels, body(): pl.pallas_call(functools.partial(kernel, n), out_shape=(pltpu.VMEM((L, R,...  20.2 us
    pallas_call x1, Pallas kernels, body(): pl.pallas_call(finish, out_shape=(jax.ShapeDtypeStruct((L, R, Q), BF16),...  1.45 us

profile of v2, /device:TPU:0, one launch (start us, length us, event | category | flops | bytes accessed | tf_op | source)
XLA Modules:
  0.0 22.3 jit_solution(18422934837800318721)
XLA Ops:
  0.6 20.2 %shard_map.86 = (bf16[8,128,128]{2,1,0:T(8,128)(2,1)S(1)}, f32[2,512,128]{2,1,0:T(8,128)S(1)}, f32[512,128]{1,0:T(8,128)S(1)}, f32[2,512,128]{2,1,0:T(8,128)S(1)}) custom-call(bf16[64,8,256]{2,1,0:T(8,128)(2,1)} %x_ref.1, bf16[64,256]{1,0:T(8,128)(2,1)} %bitcast.4, bf16[1024,128]{1,0:T(8,128)(2,1)} %wo_hbm.1, f32[1,128]{1,0:T(1,128)} %bitcast.6, ...), custom_call_target="tpu_custom_call" | custom-call | tf_op jit(solution)/shard_map/pallas_call | solution.py:295
  20.9 1.4 %shard_map.87 = (bf16[8,128,128]{2,1,0:T(8,128)(2,1)}, bf16[64,8,256]{2,1,0:T(8,128)(2,1)}) custom-call(bf16[8,128,128]{2,1,0:T(8,128)(2,1)S(1)} %get-tuple-element.6.upd_ref, f32[2,512,128]{2,1,0:T(8,128)S(1)} %get-tuple-element.7.scaled_ref, f32[512,128]{1,0:T(8,128)S(1)} %get-tuple-element.8.inv_ref, f32[2,512,128]{2,1,0:T(8,128)S(1)} %get-tuple-element.9.wide_ref), custom_call_target="tpu_custom_call" | custom-call | tf_op jit(solution)/shard_map/pallas_call | solution.py:333
